TPU v7x, 32 devices: a whole 2x2x4 slice. The times are simulated.
32 devices in a mesh: grp: 4 (over x, core), seq: 8 (over z, y).
Axes of the slice: x: 2, y: 2, z: 4, core: 2. Of those that a mesh axis runs over, the one named last changes fastest.
Arguments:
- queries: bfloat16 [1, 4096, 2048], P(None, ('grp', 'seq')), may hold values from -6 to 6
- key_vectors: bfloat16 [1, 4096, 2048], P(None, ('grp', 'seq')), may hold values from -6 to 6
- values: bfloat16 [1, 4096, 2048], P(None, ('grp', 'seq')), may hold values from -6 to 6
- log_decay: bfloat16 [1, 4096, 2048], P(None, ('grp', 'seq')), may hold values from -0.8 to 0, as said below
- write_rate: float32 [1, 16, 4096], P(None, None, ('grp', 'seq')), may hold values from 0 to 1, as said below
- out_gate: bfloat16 [1, 4096, 2048], P(None, ('grp', 'seq')), may hold values from -6 to 6
Outputs:
- layer_output: bfloat16 [1, 4096, 2048], P(None, ('grp', 'seq'))
Inputs may be any that keep to these rules, and one draw needn't show every extreme that they name: log_decay is negative. write_rate is positive.
All inputs are finite; a program needn't handle non-finite values.
Results may differ from a plain program's by a relative error of at most 0.001.
Values sent between devices are 32-bit elements; how exact they have to be, the bound alone decides.
A program may use at most 128 MiB of HBM per device.

v0:
```python
import functools
import jax
import jax.numpy as jnp
from jax import lax
from jax.experimental import pallas as pl
from jax.experimental.pallas import tpu as pltpu
from jax.sharding import PartitionSpec as P

BLOCK = 64
BATCH = 4
MESH = pl.DeviceIdType.MESH
F32 = jnp.float32
BF16 = jnp.bfloat16


def split(value):
    high = value.astype(BF16)
    return high, (value - high.astype(F32)).astype(BF16)


def mul(left, right):
    width = right.shape[1]
    lhs = jnp.concatenate(split(left), axis=1)
    parts = jnp.concatenate(split(right), axis=1)
    out = jnp.dot(lhs, jnp.concatenate([parts, parts], axis=0), preferred_element_type=F32)
    return out[:, :width] + out[:, width:]


def mul_rows(left, right):
    width = right.shape[0]
    lhs = jnp.concatenate(split(left), axis=1)
    parts = jnp.concatenate(split(right), axis=0)
    rhs = jnp.concatenate([parts, parts], axis=1)
    out = lax.dot_general(lhs, rhs, (((1,), (1,)), ((), ())), preferred_element_type=F32)
    return out[:, :width] + out[:, width:]


def mul_wide(left, right):
    high, low = split(left)
    r_high, r_low = split(right)
    lhs = jnp.concatenate([high, low], axis=1)
    rhs = jnp.concatenate([r_high, r_high], axis=0)
    return jnp.dot(lhs, rhs, preferred_element_type=F32) + jnp.dot(
        high, r_low, preferred_element_type=F32
    )


def local_terms(queries, keys, values, decays, rates):
    extent, size = queries[0].shape
    half = extent // 2
    rows = lax.broadcasted_iota(jnp.int32, (extent, extent), 0)
    cols = lax.broadcasted_iota(jnp.int32, (extent, extent), 1)
    same = (rows >= half) == (cols >= half)
    eye = jnp.where(rows == cols, 1.0, 0.0).astype(F32)
    ones = jnp.where(rows >= cols, 1.0, 0.0).astype(BF16)
    cums = [jnp.dot(ones, decay, preferred_element_type=F32) for decay in decays]
    q_f = [query.astype(F32) for query in queries]
    units = []
    for key in keys:
        key_f = key.astype(F32)
        units.append(key_f * lax.rsqrt(jnp.sum(key_f * key_f, axis=-1, keepdims=True) + 1e-06))
    pairs = []
    for query, unit, cum in zip(q_f, units, cums):
        middle = cum[half - 1 : half]
        grow = jnp.exp(cum - middle)
        pairs.append(
            mul_rows(
                jnp.concatenate([unit * grow, query * grow], axis=0), unit * jnp.exp(middle - cum)
            )
        )
    lowers, attends = [], []
    for pair, rate in zip(pairs, rates):
        lowers.append(jnp.where(rows > cols, pair[:extent] * rate, 0.0))
        attends.append(jnp.where(rows >= cols, pair[extent:] * rate, 0.0))
    diag = [jnp.where(same, lower, 0.0) for lower in lowers]
    below = [jnp.where(same, 0.0, lower) for lower in lowers]
    inverse = [eye - part for part in diag]
    power = [mul(part, part) for part in diag]
    for _ in range(half.bit_length() - 3):
        both = [mul(jnp.concatenate([x, p], axis=0), p) for x, p in zip(inverse, power)]
        inverse = [x + b[:extent] for x, b in zip(inverse, both)]
        power = [b[extent:] for b in both]
    inverse = [x + mul(x, p) for x, p in zip(inverse, power)]
    corner = [mul(x[half:], c) for x, c in zip(inverse, below)]
    corner = [mul(c, x) for c, x in zip(corner, inverse)]
    inverse = [
        jnp.concatenate([x[:half], x[half:] - c], axis=0) for x, c in zip(inverse, corner)
    ]
    from_start = [jnp.exp(cum) for cum in cums]
    carry = [
        mul_wide(x, jnp.concatenate([unit * grow, value.astype(F32)], axis=1))
        for x, unit, grow, value in zip(inverse, units, from_start, values)
    ]
    results = []
    for query, unit, cum, grow, attend, rate, carried in zip(
        q_f, units, cums, from_start, attends, rates, carry
    ):
        last = cum[extent - 1 : extent]
        key_end = jnp.transpose(unit * jnp.exp(last - cum)) * rate
        out = mul_wide(jnp.concatenate([attend, key_end], axis=0), carried)
        step_map = jnp.where(rows == cols, jnp.exp(last), 0.0) - out[extent:, :size]
        results.append(
            (
                query * grow - out[:extent, :size],
                out[:extent, size:],
                jnp.concatenate([step_map, out[extent:, size:]], axis=1),
            )
        )
    return results


def kernel(
    groups, count, heads,
    q_ref, k_ref, v_ref, d_ref, r_ref, g_ref, o_ref,
    sent, arrived, prior, entry, onward, starts, begin, reach, local,
    up_send, up_recv, chain_send, chain_recv, down_send, down_recv,
):
    grp, me = lax.axis_index("grp"), lax.axis_index("seq")
    per = max(heads // count, 1)
    owners = heads // per
    extent = q_ref.shape[0]
    size = q_ref.shape[1] // heads
    everyone = owners == count

    def when_owner(body):
        if everyone:
            body()
        else:
            pl.when(me < owners)(body)

    barrier = pltpu.get_barrier_semaphore()

    def greet(step, _):
        peer = lax.rem(me + step, count)
        pl.semaphore_signal(barrier, inc=1, device_id=(grp, peer), device_id_type=MESH)
        return 0

    lax.fori_loop(1, count, greet, 0)

    @pl.when(grp > 0)
    def _():
        pl.semaphore_signal(barrier, inc=1, device_id=(grp - 1, me), device_id_type=MESH)

    @pl.when(grp < groups - 1)
    def _():
        pl.semaphore_signal(barrier, inc=1, device_id=(grp + 1, me), device_id_type=MESH)

    beside = jnp.minimum(grp, 1) + jnp.minimum(groups - 1 - grp, 1)
    pl.semaphore_wait(barrier, count - 1 + beside)

    def columns(head):
        return pl.ds(pl.multiple_of(head * size, size), size)

    def up_copy(head, shard, owner):
        return pltpu.make_async_remote_copy(
            src_ref=sent.at[head],
            dst_ref=arrived.at[shard, lax.rem(head, per)],
            send_sem=up_send.at[head],
            recv_sem=up_recv.at[shard, lax.rem(head, per)],
            device_id=(grp, owner),
            device_id_type=MESH,
        )

    def compute(step, _):
        picked = [
            lax.rem(step * BATCH + index + per * (me + 1), heads) for index in range(BATCH)
        ]
        spans = [columns(head) for head in picked]
        results = local_terms(
            [q_ref[:, span] for span in spans],
            [k_ref[:, span] for span in spans],
            [v_ref[:, span] for span in spans],
            [d_ref[:, span] for span in spans],
            [r_ref[pl.ds(head, 1), :] for head in picked],
        )
        for head, (head_reach, head_local, head_step) in zip(picked, results):
            reach[head] = head_reach
            local[head] = head_local
            sent[head] = head_step
            owner = lax.div(head, per)

            @pl.when(owner != me)
            def _():
                up_copy(head, me, owner).start()

            @pl.when(owner == me)
            def _():
                arrived[me, lax.rem(head, per)] = head_step

        return 0

    lax.fori_loop(0, heads // BATCH, compute, 0)

    rows = lax.broadcasted_iota(jnp.int32, (size, 2 * size), 0)
    cols = lax.broadcasted_iota(jnp.int32, (size, 2 * size), 1)

    def compose():
        for index in range(per):
            prior[0, index] = jnp.where(rows == cols, 1.0, 0.0).astype(F32)

        def advance(shard, _):
            @pl.when(shard != me)
            def _():
                for index in range(per):
                    up_copy(me * per + index, shard, me).wait_recv()

            for index in range(per):
                step = arrived[shard, index]
                product = mul_wide(step[:, :size], prior[shard, index])
                prior[shard + 1, index, :, :size] = product[:, :size]
                prior[shard + 1, index, :, size:] = product[:, size:] + step[:, size:]
            return 0

        lax.fori_loop(0, count, advance, 0)

        def chain_copy(target):
            return pltpu.make_async_remote_copy(
                src_ref=onward,
                dst_ref=entry,
                send_sem=chain_send,
                recv_sem=chain_recv,
                device_id=(target, me),
                device_id_type=MESH,
            )

        @pl.when(grp == 0)
        def _():
            entry[...] = jnp.zeros_like(entry)

        @pl.when(grp > 0)
        def _():
            chain_copy(grp).wait_recv()

        @pl.when(grp < groups - 1)
        def _():
            for index in range(per):
                total = prior[count, index]
                onward[index] = mul(total[:, :size], entry[index]) + total[:, size:]
            chain_copy(grp + 1).start()

        def give(step, _):
            shard = lax.rem(me + 1 + step, count)
            for index in range(per):
                before = prior[shard, index]
                starts[shard, index] = mul(before[:, :size], entry[index]) + before[:, size:]

            @pl.when(shard != me)
            def _():
                down_copy(shard, me).start()

            @pl.when(shard == me)
            def _():
                begin[pl.ds(me * per, per)] = starts[shard]

            return 0

        lax.fori_loop(0, count, give, 0)

        @pl.when(grp < groups - 1)
        def _():
            chain_copy(grp + 1).wait_send()

    def down_copy(shard, owner):
        return pltpu.make_async_remote_copy(
            src_ref=starts.at[shard],
            dst_ref=begin.at[pl.ds(owner * per, per)],
            send_sem=down_send.at[shard],
            recv_sem=down_recv.at[owner],
            device_id=(grp, shard),
            device_id_type=MESH,
        )

    when_owner(compose)

    def finish(step, _):
        owner = lax.rem(me + owners - step, owners) if everyone else step

        @pl.when(owner != me)
        def _():
            down_copy(me, owner).wait_recv()

        for index in range(per):
            head = owner * per + index
            raw = mul(reach[head], begin[head]) + local[head]
            scaled = raw * lax.rsqrt(jnp.mean(raw * raw, axis=-1, keepdims=True) + 1e-05)
            gate = g_ref[:, columns(head)].astype(F32)
            o_ref[:, columns(head)] = (scaled / (1.0 + jnp.exp(-gate))).astype(BF16)
        return 0

    lax.fori_loop(0, owners, finish, 0)

    def drain_up(head, _):
        owner = lax.div(head, per)

        @pl.when(owner != me)
        def _():
            up_copy(head, me, owner).wait_send()

        return 0

    lax.fori_loop(0, heads, drain_up, 0)

    def drain_down():
        def one(shard, _):
            @pl.when(shard != me)
            def _():
                down_copy(shard, me).wait_send()

            return 0

        lax.fori_loop(0, count, one, 0)

    when_owner(drain_down)


def shards(groups, count, queries, key_vectors, values, log_decay, write_rate, out_gate):
    seq_count, local_len, features = queries.shape
    heads = write_rate.shape[1]
    size = features // heads
    per = max(heads // count, 1)
    dma = pltpu.SemaphoreType.DMA
    square = (size, size)
    wide = (size, 2 * size)
    call = pl.pallas_call(
        functools.partial(kernel, groups, count, heads),
        out_shape=jax.ShapeDtypeStruct((local_len, features), BF16),
        in_specs=[pl.BlockSpec(memory_space=pltpu.VMEM)] * 6,
        out_specs=pl.BlockSpec(memory_space=pltpu.VMEM),
        scratch_shapes=[
            pltpu.VMEM((heads, *wide), F32),
            pltpu.VMEM((count, per, *wide), F32),
            pltpu.VMEM((count + 1, per, *wide), F32),
            pltpu.VMEM((per, *square), F32),
            pltpu.VMEM((per, *square), F32),
            pltpu.VMEM((count, per, *square), F32),
            pltpu.VMEM((heads, *square), F32),
            pltpu.VMEM((heads, local_len, size), F32),
            pltpu.VMEM((heads, local_len, size), F32),
            dma((heads,)),
            dma((count, per)),
            dma,
            dma,
            dma((count,)),
            dma((heads // per,)),
        ],
        compiler_params=pltpu.CompilerParams(
            collective_id=0, has_side_effects=True, vmem_limit_bytes=48 * 1024 * 1024
        ),
        name="delta_attention",
    )
    result = call(
        queries[0], key_vectors[0], values[0], log_decay[0], write_rate[0], out_gate[0]
    )
    return result[None]


def solution(mesh):
    spread = P(None, ("grp", "seq"), None)
    return jax.shard_map(
        functools.partial(shards, mesh.shape["grp"], mesh.shape["seq"]),
        mesh=mesh,
        in_specs=(spread, spread, spread, spread, P(None, None, ("grp", "seq")), spread),
        out_specs=spread,
        check_vma=False,
    )
```

profile of v0, /device:TPU:23, one launch (start us, length us, event | category | flops | bytes accessed | tf_op | source)
XLA Modules:
  0.0 98.5 jit_solution(7637057947922869329)
XLA Ops:
  0.0 0.0 copy-start.5
  0.0 0.7 copy-done.5
  0.7 0.0 copy-start
  0.7 1.0 %copy-done = bf16[1,128,2048]{2,1,0:T(8,128)(2,1)S(1)} copy-done((bf16[1,128,2048]{2,1,0:T(8,128)(2,1)S(1)}, bf16[1,128,2048]{2,1,0:T(8,128)(2,1)}, u32[]{:S(2)}) %copy-start) | copy-done | bytes 524312
  1.7 0.0 copy-start.1
  1.7 1.0 %copy-done.1 = bf16[1,128,2048]{2,1,0:T(8,128)(2,1)S(1)} copy-done((bf16[1,128,2048]{2,1,0:T(8,128)(2,1)S(1)}, bf16[1,128,2048]{2,1,0:T(8,128)(2,1)}, u32[]{:S(2)}) %copy-start.1) | copy-done | bytes 524312
  2.8 0.0 copy-start.2
  2.8 1.0 %copy-done.2 = bf16[1,128,2048]{2,1,0:T(8,128)(2,1)S(1)} copy-done((bf16[1,128,2048]{2,1,0:T(8,128)(2,1)S(1)}, bf16[1,128,2048]{2,1,0:T(8,128)(2,1)}, u32[]{:S(2)}) %copy-start.2) | copy-done | bytes 524312
  3.8 0.0 copy-start.3
  3.8 1.0 %copy-done.3 = bf16[1,128,2048]{2,1,0:T(8,128)(2,1)S(1)} copy-done((bf16[1,128,2048]{2,1,0:T(8,128)(2,1)S(1)}, bf16[1,128,2048]{2,1,0:T(8,128)(2,1)}, u32[]{:S(2)}) %copy-start.3) | copy-done | bytes 524312
  4.9 0.0 copy-start.4
  4.9 1.0 %copy-done.4 = bf16[1,128,2048]{2,1,0:T(8,128)(2,1)S(1)} copy-done((bf16[1,128,2048]{2,1,0:T(8,128)(2,1)S(1)}, bf16[1,128,2048]{2,1,0:T(8,128)(2,1)}, u32[]{:S(2)}) %copy-start.4) | copy-done | bytes 524312
  5.9 91.8 %delta_attention.1 = bf16[128,2048]{1,0:T(8,128)(2,1)S(1)} custom-call(bf16[128,2048]{1,0:T(8,128)(2,1)S(1)} %bitcast.8, bf16[128,2048]{1,0:T(8,128)(2,1)S(1)} %bitcast.9, bf16[128,2048]{1,0:T(8,128)(2,1)S(1)} %bitcast.10, bf16[128,2048]{1,0:T(8,128)(2,1)S(1)} %bitcast.11, f32[16,128]{1,0:T(8,128)S(1)} %bitcast.13, bf16[128,2048]{1,0:T(8,128)(2,1)S(1)} %bitcast.12), custom_call_target="tpu_custom_call" | custom-call | tf_op jit(solution)/shard_map/delta_attention/pallas_call | solution.py:351
  97.7 0.8 copy.8
Async XLA Ops:
  0.0 0.7 copy-start.5
  0.7 1.0 %copy-start = (bf16[1,128,2048]{2,1,0:T(8,128)(2,1)S(1)}, bf16[1,128,2048]{2,1,0:T(8,128)(2,1)}, u32[]{:S(2)}) copy-start(bf16[1,128,2048]{2,1,0:T(8,128)(2,1)} %param.6) | copy-start | bytes 1572868
  1.7 1.0 %copy-start.1 = (bf16[1,128,2048]{2,1,0:T(8,128)(2,1)S(1)}, bf16[1,128,2048]{2,1,0:T(8,128)(2,1)}, u32[]{:S(2)}) copy-start(bf16[1,128,2048]{2,1,0:T(8,128)(2,1)} %param.7) | copy-start | bytes 1572868
  2.8 1.0 %copy-start.2 = (bf16[1,128,2048]{2,1,0:T(8,128)(2,1)S(1)}, bf16[1,128,2048]{2,1,0:T(8,128)(2,1)}, u32[]{:S(2)}) copy-start(bf16[1,128,2048]{2,1,0:T(8,128)(2,1)} %param.8) | copy-start | bytes 1572868
  3.8 1.0 %copy-start.3 = (bf16[1,128,2048]{2,1,0:T(8,128)(2,1)S(1)}, bf16[1,128,2048]{2,1,0:T(8,128)(2,1)}, u32[]{:S(2)}) copy-start(bf16[1,128,2048]{2,1,0:T(8,128)(2,1)} %param.9) | copy-start | bytes 1572868
  4.9 1.0 %copy-start.4 = (bf16[1,128,2048]{2,1,0:T(8,128)(2,1)S(1)}, bf16[1,128,2048]{2,1,0:T(8,128)(2,1)}, u32[]{:S(2)}) copy-start(bf16[1,128,2048]{2,1,0:T(8,128)(2,1)} %param.11) | copy-start | bytes 1572868
where the time goes:
time: 98.9 us; the launch traced here: 98.5 us
  Pallas kernels  91.8 us (93%)
  local copies, waits for them, and re-layouts  6.7 us (7%)
    pallas_call x1, Pallas kernels, shards(): call(queries[0], key_vectors[0], values[0], log_decay[0], write_rate[0],...  91.8 us
    unnamed x13, local copies, waits for them, and re-layouts  6.7 us

commit v1 on v0

--- a/solution.py
+++ b/solution.py
@@ -111,9 +111,11 @@
 
 def kernel(
     groups, count, heads,
-    q_ref, k_ref, v_ref, d_ref, r_ref, g_ref, o_ref,
-    sent, arrived, prior, entry, onward, starts, begin, reach, local,
-    up_send, up_recv, chain_send, chain_recv, down_send, down_recv,
+    q_hbm, k_hbm, v_hbm, d_hbm, g_hbm, r_ref, o_hbm,
+    q_ref, k_ref, v_ref, d_ref, g_ref, o_ref,
+    sent, arrived, prior, total_in, pair_in, entry, onward, starts, begin, reach, local,
+    load_sem, gate_sem, store_sem,
+    up_send, up_recv, total_send, total_recv, pair_send, pair_recv, down_send, down_recv,
 ):
     grp, me = lax.axis_index("grp"), lax.axis_index("seq")
     per = max(heads // count, 1)
@@ -121,6 +123,10 @@
     extent = q_ref.shape[0]
     size = q_ref.shape[1] // heads
     everyone = owners == count
+    batches = heads // BATCH
+    first_batch = lax.div(per * me, BATCH) + 1
+    pair, odd = lax.div(grp, 2), lax.rem(grp, 2)
+    last_pair = groups // 2 - 1
 
     def when_owner(body):
         if everyone:
@@ -128,24 +134,58 @@
         else:
             pl.when(me < owners)(body)
 
+    def greet_at(group, seq):
+        pl.semaphore_signal(barrier, inc=1, device_id=(group, seq), device_id_type=MESH)
+
     barrier = pltpu.get_barrier_semaphore()
 
     def greet(step, _):
-        peer = lax.rem(me + step, count)
-        pl.semaphore_signal(barrier, inc=1, device_id=(grp, peer), device_id_type=MESH)
+        greet_at(grp, lax.rem(me + step, count))
         return 0
 
     lax.fori_loop(1, count, greet, 0)
 
-    @pl.when(grp > 0)
+    @pl.when(odd == 0)
     def _():
-        pl.semaphore_signal(barrier, inc=1, device_id=(grp - 1, me), device_id_type=MESH)
-
-    @pl.when(grp < groups - 1)
+        greet_at(grp + 1, me)
+
+    @pl.when(odd == 1)
     def _():
-        pl.semaphore_signal(barrier, inc=1, device_id=(grp + 1, me), device_id_type=MESH)
-
-    beside = jnp.minimum(grp, 1) + jnp.minimum(groups - 1 - grp, 1)
+        greet_at(grp - 1, me)
+
+    @pl.when(jnp.logical_and(odd == 0, pair > 0))
+    def _():
+        greet_at(grp - 1, me)
+
+    @pl.when(jnp.logical_and(odd == 1, pair > 0))
+    def _():
+        greet_at(grp - 2, me)
+
+    @pl.when(jnp.logical_and(odd == 1, pair < last_pair))
+    def _():
+        greet_at(grp + 1, me)
+        greet_at(grp + 2, me)
+
+    def batch_columns(step):
+        batch = lax.rem(step + first_batch, batches)
+        return batch, pl.ds(pl.multiple_of(batch * (BATCH * size), BATCH * size), BATCH * size)
+
+    def load(step):
+        batch, span = batch_columns(step)
+        return [
+            pltpu.make_async_copy(far.at[:, span], near.at[:, span], load_sem.at[index, batch])
+            for index, (far, near) in enumerate(
+                [(d_hbm, d_ref), (k_hbm, k_ref), (q_hbm, q_ref), (v_hbm, v_ref)]
+            )
+        ]
+
+    for step in range(batches):
+        for copy in load(step):
+            copy.start()
+    gate_copy = pltpu.make_async_copy(g_hbm, g_ref, gate_sem)
+    gate_copy.start()
+
+    beside = 1 + jnp.minimum(pair, 1) + 2 * odd * jnp.minimum(last_pair - pair, 1)
     pl.semaphore_wait(barrier, count - 1 + beside)
 
     def columns(head):
@@ -162,9 +202,10 @@
         )
 
     def compute(step, _):
-        picked = [
-            lax.rem(step * BATCH + index + per * (me + 1), heads) for index in range(BATCH)
-        ]
+        for copy in load(step):
+            copy.wait()
+        batch, _unused = batch_columns(step)
+        picked = [batch * BATCH + index for index in range(BATCH)]
         spans = [columns(head) for head in picked]
         results = local_terms(
             [q_ref[:, span] for span in spans],
@@ -189,76 +230,37 @@
 
         return 0
 
-    lax.fori_loop(0, heads // BATCH, compute, 0)
+    lax.fori_loop(0, batches, compute, 0)
 
     rows = lax.broadcasted_iota(jnp.int32, (size, 2 * size), 0)
     cols = lax.broadcasted_iota(jnp.int32, (size, 2 * size), 1)
 
-    def compose():
-        for index in range(per):
-            prior[0, index] = jnp.where(rows == cols, 1.0, 0.0).astype(F32)
-
-        def advance(shard, _):
-            @pl.when(shard != me)
-            def _():
-                for index in range(per):
-                    up_copy(me * per + index, shard, me).wait_recv()
-
-            for index in range(per):
-                step = arrived[shard, index]
-                product = mul_wide(step[:, :size], prior[shard, index])
-                prior[shard + 1, index, :, :size] = product[:, :size]
-                prior[shard + 1, index, :, size:] = product[:, size:] + step[:, size:]
-            return 0
-
-        lax.fori_loop(0, count, advance, 0)
-
-        def chain_copy(target):
-            return pltpu.make_async_remote_copy(
-                src_ref=onward,
-                dst_ref=entry,
-                send_sem=chain_send,
-                recv_sem=chain_recv,
-                device_id=(target, me),
-                device_id_type=MESH,
-            )
-
-        @pl.when(grp == 0)
-        def _():
-            entry[...] = jnp.zeros_like(entry)
-
-        @pl.when(grp > 0)
-        def _():
-            chain_copy(grp).wait_recv()
-
-        @pl.when(grp < groups - 1)
-        def _():
-            for index in range(per):
-                total = prior[count, index]
-                onward[index] = mul(total[:, :size], entry[index]) + total[:, size:]
-            chain_copy(grp + 1).start()
-
-        def give(step, _):
-            shard = lax.rem(me + 1 + step, count)
-            for index in range(per):
-                before = prior[shard, index]
-                starts[shard, index] = mul(before[:, :size], entry[index]) + before[:, size:]
-
-            @pl.when(shard != me)
-            def _():
-                down_copy(shard, me).start()
-
-            @pl.when(shard == me)
-            def _():
-                begin[pl.ds(me * per, per)] = starts[shard]
-
-            return 0
-
-        lax.fori_loop(0, count, give, 0)
-
-        @pl.when(grp < groups - 1)
-        def _():
-            chain_copy(grp + 1).wait_send()
+    def join(late, early):
+        product = mul_wide(late[:, :size], early)
+        return product[:, :size], product[:, size:] + late[:, size:]
+
+    def apply(step, state):
+        return mul(step[:, :size], state) + step[:, size:]
+
+    def total_copy(target):
+        return pltpu.make_async_remote_copy(
+            src_ref=prior.at[count],
+            dst_ref=total_in,
+            send_sem=total_send,
+            recv_sem=total_recv,
+            device_id=(target, me),
+            device_id_type=MESH,
+        )
+
+    def pair_copy(ahead):
+        return pltpu.make_async_remote_copy(
+            src_ref=onward,
+            dst_ref=pair_in,
+            send_sem=pair_send.at[ahead - 1],
+            recv_sem=pair_recv,
+            device_id=(grp + ahead, me),
+            device_id_type=MESH,
+        )
 
     def down_copy(shard, owner):
         return pltpu.make_async_remote_copy(
@@ -270,7 +272,83 @@
             device_id_type=MESH,
         )
 
+    def compose():
+        for index in range(per):
+            prior[0, index] = jnp.where(rows == cols, 1.0, 0.0).astype(F32)
+
+        def advance(shard, _):
+            @pl.when(shard != me)
+            def _():
+                for index in range(per):
+                    up_copy(me * per + index, shard, me).wait_recv()
+
+            for index in range(per):
+                whole, added = join(arrived[shard, index], prior[shard, index])
+                prior[shard + 1, index, :, :size] = whole
+                prior[shard + 1, index, :, size:] = added
+            return 0
+
+        lax.fori_loop(0, count, advance, 0)
+
+        @pl.when(odd == 0)
+        def _():
+            total_copy(grp + 1).start()
+
+        @pl.when(pair == 0)
+        def _():
+            pair_in[...] = jnp.zeros_like(pair_in)
+
+        @pl.when(odd == 1)
+        def _():
+            total_copy(grp).wait_recv()
+            both = [join(prior[count, index], total_in[index]) for index in range(per)]
+
+            @pl.when(pair > 0)
+            def _():
+                pair_copy(1).wait_recv()
+
+            for index in range(per):
+                onward[index] = mul(both[index][0], pair_in[index]) + both[index][1]
+
+            @pl.when(pair < last_pair)
+            def _():
+                pair_copy(2).start()
+                pair_copy(1).start()
+
+            for index in range(per):
+                entry[index] = apply(total_in[index], pair_in[index])
+
+        @pl.when(odd == 0)
+        def _():
+            @pl.when(pair > 0)
+            def _():
+                pair_copy(1).wait_recv()
+
+            entry[...] = pair_in[...]
+
+        def give(step, _):
+            shard = lax.rem(me + 1 + step, count)
+            for index in range(per):
+                starts[shard, index] = apply(prior[shard, index], entry[index])
+
+            @pl.when(shard != me)
+            def _():
+                down_copy(shard, me).start()
+
+            @pl.when(shard == me)
+            def _():
+                begin[pl.ds(me * per, per)] = starts[shard]
+
+            return 0
+
+        lax.fori_loop(0, count, give, 0)
+
     when_owner(compose)
+    gate_copy.wait()
+
+    def store(owner):
+        span = pl.ds(pl.multiple_of(owner * (per * size), per * size), per * size)
+        return pltpu.make_async_copy(o_ref.at[:, span], o_hbm.at[:, span], store_sem.at[owner])
 
     def finish(step, _):
         owner = lax.rem(me + owners - step, owners) if everyone else step
@@ -285,6 +363,7 @@
             scaled = raw * lax.rsqrt(jnp.mean(raw * raw, axis=-1, keepdims=True) + 1e-05)
             gate = g_ref[:, columns(head)].astype(F32)
             o_ref[:, columns(head)] = (scaled / (1.0 + jnp.exp(-gate))).astype(BF16)
+        store(owner).start()
         return 0
 
     lax.fori_loop(0, owners, finish, 0)
@@ -301,6 +380,15 @@
     lax.fori_loop(0, heads, drain_up, 0)
 
     def drain_down():
+        @pl.when(odd == 0)
+        def _():
+            total_copy(grp + 1).wait_send()
+
+        @pl.when(jnp.logical_and(odd == 1, pair < last_pair))
+        def _():
+            pair_copy(2).wait_send()
+            pair_copy(1).wait_send()
+
         def one(shard, _):
             @pl.when(shard != me)
             def _():
@@ -311,6 +399,12 @@
         lax.fori_loop(0, count, one, 0)
 
     when_owner(drain_down)
+
+    def drain_store(owner, _):
+        store(owner).wait()
+        return 0
+
+    lax.fori_loop(0, owners, drain_store, 0)
 
 
 def shards(groups, count, queries, key_vectors, values, log_decay, write_rate, out_gate):
@@ -324,21 +418,30 @@
     call = pl.pallas_call(
         functools.partial(kernel, groups, count, heads),
         out_shape=jax.ShapeDtypeStruct((local_len, features), BF16),
-        in_specs=[pl.BlockSpec(memory_space=pltpu.VMEM)] * 6,
-        out_specs=pl.BlockSpec(memory_space=pltpu.VMEM),
-        scratch_shapes=[
+        in_specs=[pl.BlockSpec(memory_space=pltpu.HBM)] * 5
+        + [pl.BlockSpec(memory_space=pltpu.VMEM)],
+        out_specs=pl.BlockSpec(memory_space=pltpu.HBM),
+        scratch_shapes=[pltpu.VMEM((local_len, features), BF16)] * 6
+        + [
             pltpu.VMEM((heads, *wide), F32),
             pltpu.VMEM((count, per, *wide), F32),
             pltpu.VMEM((count + 1, per, *wide), F32),
+            pltpu.VMEM((per, *wide), F32),
+            pltpu.VMEM((per, *square), F32),
             pltpu.VMEM((per, *square), F32),
             pltpu.VMEM((per, *square), F32),
             pltpu.VMEM((count, per, *square), F32),
             pltpu.VMEM((heads, *square), F32),
             pltpu.VMEM((heads, local_len, size), F32),
             pltpu.VMEM((heads, local_len, size), F32),
+            dma((4, heads // BATCH)),
+            dma,
+            dma((heads // per,)),
             dma((heads,)),
             dma((count, per)),
             dma,
+            dma,
+            dma((2,)),
             dma,
             dma((count,)),
             dma((heads // per,)),
@@ -349,7 +452,7 @@
         name="delta_attention",
     )
     result = call(
-        queries[0], key_vectors[0], values[0], log_decay[0], write_rate[0], out_gate[0]
+        queries[0], key_vectors[0], values[0], log_decay[0], out_gate[0], write_rate[0]
     )
     return result[None]
 

time: 98.9 us -> 98.7 us (level)
  the two profiles are of different devices: /device:TPU:23 before, /device:TPU:22 now
where the time goes in v1:
time: 98.7 us; the launch traced here: 98.4 us
  Pallas kernels  91.6 us (93%)
  local copies, waits for them, and re-layouts  6.7 us (7%)
    pallas_call x1, Pallas kernels, shards(): call(queries[0], key_vectors[0], values[0], log_decay[0], out_gate[0], wr...  91.6 us
    unnamed x13, local copies, waits for them, and re-layouts  6.7 us

profile of v1, /device:TPU:22, one launch (start us, length us, event | category | flops | bytes accessed | tf_op | source)
XLA Modules:
  0.0 98.4 jit_solution(239716889207262747)
XLA Ops:
  0.0 0.0 copy-start.5
  0.0 0.7 copy-done.5
  0.7 0.0 copy-start
  0.7 1.0 %copy-done = bf16[1,128,2048]{2,1,0:T(8,128)(2,1)S(1)} copy-done((bf16[1,128,2048]{2,1,0:T(8,128)(2,1)S(1)}, bf16[1,128,2048]{2,1,0:T(8,128)(2,1)}, u32[]{:S(2)}) %copy-start) | copy-done | bytes 524312
  1.7 0.0 copy-start.1
  1.7 1.0 %copy-done.1 = bf16[1,128,2048]{2,1,0:T(8,128)(2,1)S(1)} copy-done((bf16[1,128,2048]{2,1,0:T(8,128)(2,1)S(1)}, bf16[1,128,2048]{2,1,0:T(8,128)(2,1)}, u32[]{:S(2)}) %copy-start.1) | copy-done | bytes 524312
  2.8 0.0 copy-start.2
  2.8 1.0 %copy-done.2 = bf16[1,128,2048]{2,1,0:T(8,128)(2,1)S(1)} copy-done((bf16[1,128,2048]{2,1,0:T(8,128)(2,1)S(1)}, bf16[1,128,2048]{2,1,0:T(8,128)(2,1)}, u32[]{:S(2)}) %copy-start.2) | copy-done | bytes 524312
  3.8 0.0 copy-start.3
  3.8 1.0 %copy-done.3 = bf16[1,128,2048]{2,1,0:T(8,128)(2,1)S(1)} copy-done((bf16[1,128,2048]{2,1,0:T(8,128)(2,1)S(1)}, bf16[1,128,2048]{2,1,0:T(8,128)(2,1)}, u32[]{:S(2)}) %copy-start.3) | copy-done | bytes 524312
  4.9 0.0 copy-start.4
  4.9 1.0 %copy-done.4 = bf16[1,128,2048]{2,1,0:T(8,128)(2,1)S(1)} copy-done((bf16[1,128,2048]{2,1,0:T(8,128)(2,1)S(1)}, bf16[1,128,2048]{2,1,0:T(8,128)(2,1)}, u32[]{:S(2)}) %copy-start.4) | copy-done | bytes 524312
  5.9 91.6 %delta_attention.1 = bf16[128,2048]{1,0:T(8,128)(2,1)S(1)} custom-call(bf16[128,2048]{1,0:T(8,128)(2,1)S(1)} %bitcast.8, bf16[128,2048]{1,0:T(8,128)(2,1)S(1)} %bitcast.9, bf16[128,2048]{1,0:T(8,128)(2,1)S(1)} %bitcast.10, bf16[128,2048]{1,0:T(8,128)(2,1)S(1)} %bitcast.11, bf16[128,2048]{1,0:T(8,128)(2,1)S(1)} %bitcast.12, f32[16,128]{1,0:T(8,128)S(1)} %bitcast.13), custom_call_target="tpu_custom_call" | custom-call | tf_op jit(solution)/shard_map/delta_attention/pallas_call | solution.py:454
  97.6 0.8 copy.8
Async XLA Ops:
  0.0 0.7 copy-start.5
  0.7 1.0 %copy-start = (bf16[1,128,2048]{2,1,0:T(8,128)(2,1)S(1)}, bf16[1,128,2048]{2,1,0:T(8,128)(2,1)}, u32[]{:S(2)}) copy-start(bf16[1,128,2048]{2,1,0:T(8,128)(2,1)} %param.6) | copy-start | bytes 1572868
  1.7 1.0 %copy-start.1 = (bf16[1,128,2048]{2,1,0:T(8,128)(2,1)S(1)}, bf16[1,128,2048]{2,1,0:T(8,128)(2,1)}, u32[]{:S(2)}) copy-start(bf16[1,128,2048]{2,1,0:T(8,128)(2,1)} %param.7) | copy-start | bytes 1572868
  2.8 1.0 %copy-start.2 = (bf16[1,128,2048]{2,1,0:T(8,128)(2,1)S(1)}, bf16[1,128,2048]{2,1,0:T(8,128)(2,1)}, u32[]{:S(2)}) copy-start(bf16[1,128,2048]{2,1,0:T(8,128)(2,1)} %param.8) | copy-start | bytes 1572868
  3.8 1.0 %copy-start.3 = (bf16[1,128,2048]{2,1,0:T(8,128)(2,1)S(1)}, bf16[1,128,2048]{2,1,0:T(8,128)(2,1)}, u32[]{:S(2)}) copy-start(bf16[1,128,2048]{2,1,0:T(8,128)(2,1)} %param.9) | copy-start | bytes 1572868
  4.9 1.0 %copy-start.4 = (bf16[1,128,2048]{2,1,0:T(8,128)(2,1)S(1)}, bf16[1,128,2048]{2,1,0:T(8,128)(2,1)}, u32[]{:S(2)}) copy-start(bf16[1,128,2048]{2,1,0:T(8,128)(2,1)} %param.11) | copy-start | bytes 1572868

commit v2 on v1

--- a/solution.py
+++ b/solution.py
@@ -113,18 +113,22 @@
     groups, count, heads,
     q_hbm, k_hbm, v_hbm, d_hbm, g_hbm, r_ref, o_hbm,
     q_ref, k_ref, v_ref, d_ref, g_ref, o_ref,
-    sent, arrived, prior, total_in, pair_in, entry, onward, starts, begin, reach, local,
-    load_sem, gate_sem, store_sem,
-    up_send, up_recv, total_send, total_recv, pair_send, pair_recv, down_send, down_recv,
+    outgo, duo, comp, arrived, prior, total_in, pair_in, entry, onward, starts, slots, begin,
+    reach, local,
+    load_sem, gate_sem, store_sem, mate_send, mate_recv, up_send, up_recv,
+    total_send, total_recv, pair_send, pair_recv, down_send, down_recv, relay_send, relay_recv,
 ):
     grp, me = lax.axis_index("grp"), lax.axis_index("seq")
     per = max(heads // count, 1)
     owners = heads // per
-    extent = q_ref.shape[0]
     size = q_ref.shape[1] // heads
     everyone = owners == count
-    batches = heads // BATCH
-    first_batch = lax.div(per * me, BATCH) + 1
+    places, hosts = count // 2, owners // 2
+    place, side = lax.div(me, 2), lax.rem(me, 2)
+    mate = me + 1 - 2 * side
+    turns = heads // 2 // BATCH
+    runs = BATCH // per
+    first_turn = lax.div(per * place, BATCH) + 1
     pair, odd = lax.div(grp, 2), lax.rem(grp, 2)
     last_pair = groups // 2 - 1
 
@@ -138,12 +142,13 @@
         pl.semaphore_signal(barrier, inc=1, device_id=(group, seq), device_id_type=MESH)
 
     barrier = pltpu.get_barrier_semaphore()
+    greet_at(grp, mate)
 
     def greet(step, _):
-        greet_at(grp, lax.rem(me + step, count))
-        return 0
-
-    lax.fori_loop(1, count, greet, 0)
+        greet_at(grp, lax.rem(me + 2 * step, count))
+        return 0
+
+    lax.fori_loop(1, places, greet, 0)
 
     @pl.when(odd == 0)
     def _():
@@ -166,46 +171,50 @@
         greet_at(grp + 1, me)
         greet_at(grp + 2, me)
 
-    def batch_columns(step):
-        batch = lax.rem(step + first_batch, batches)
-        return batch, pl.ds(pl.multiple_of(batch * (BATCH * size), BATCH * size), BATCH * size)
-
-    def load(step):
-        batch, span = batch_columns(step)
+    def turn_owners(turn, whose):
+        start = lax.rem(turn + first_turn, turns) * runs
+        return [2 * (start + run) + whose for run in range(runs)]
+
+    def owner_columns(owner):
+        return pl.ds(pl.multiple_of(owner * (per * size), per * size), per * size)
+
+    def load(owner):
+        span = owner_columns(owner)
         return [
-            pltpu.make_async_copy(far.at[:, span], near.at[:, span], load_sem.at[index, batch])
+            pltpu.make_async_copy(far.at[:, span], near.at[:, span], load_sem.at[index, owner])
             for index, (far, near) in enumerate(
                 [(d_hbm, d_ref), (k_hbm, k_ref), (q_hbm, q_ref), (v_hbm, v_ref)]
             )
         ]
 
-    for step in range(batches):
-        for copy in load(step):
-            copy.start()
+    for whose in (1 - side, side):
+        for turn in range(turns):
+            for owner in turn_owners(turn, whose):
+                for copy in load(owner):
+                    copy.start()
     gate_copy = pltpu.make_async_copy(g_hbm, g_ref, gate_sem)
     gate_copy.start()
 
     beside = 1 + jnp.minimum(pair, 1) + 2 * odd * jnp.minimum(last_pair - pair, 1)
-    pl.semaphore_wait(barrier, count - 1 + beside)
+    pl.semaphore_wait(barrier, places + beside)
 
     def columns(head):
         return pl.ds(pl.multiple_of(head * size, size), size)
 
-    def up_copy(head, shard, owner):
-        return pltpu.make_async_remote_copy(
-            src_ref=sent.at[head],
-            dst_ref=arrived.at[shard, lax.rem(head, per)],
-            send_sem=up_send.at[head],
-            recv_sem=up_recv.at[shard, lax.rem(head, per)],
-            device_id=(grp, owner),
-            device_id_type=MESH,
-        )
-
-    def compute(step, _):
-        for copy in load(step):
-            copy.wait()
-        batch, _unused = batch_columns(step)
-        picked = [batch * BATCH + index for index in range(BATCH)]
+    def join(late, early):
+        product = mul_wide(late[:, :size], early)
+        return product[:, :size], product[:, size:] + late[:, size:]
+
+    def apply(step, state):
+        return mul(step[:, :size], state) + step[:, size:]
+
+    def compute(turn, whose):
+        turn_of = turn_owners(turn, whose)
+        for owner in turn_of:
+            for copy in load(owner):
+                copy.wait()
+        picked = [owner * per + index for owner in turn_of for index in range(per)]
+        places_in = [lax.div(owner, 2) * per + index for owner in turn_of for index in range(per)]
         spans = [columns(head) for head in picked]
         results = local_terms(
             [q_ref[:, span] for span in spans],
@@ -214,37 +223,70 @@
             [d_ref[:, span] for span in spans],
             [r_ref[pl.ds(head, 1), :] for head in picked],
         )
-        for head, (head_reach, head_local, head_step) in zip(picked, results):
+        for head, (head_reach, head_local, _step) in zip(picked, results):
             reach[head] = head_reach
             local[head] = head_local
-            sent[head] = head_step
-            owner = lax.div(head, per)
-
-            @pl.when(owner != me)
-            def _():
-                up_copy(head, me, owner).start()
-
-            @pl.when(owner == me)
-            def _():
-                arrived[me, lax.rem(head, per)] = head_step
-
-        return 0
-
-    lax.fori_loop(0, batches, compute, 0)
+        return places_in, [result[2] for result in results]
+
+    def mate_copy(spot, slot):
+        return pltpu.make_async_remote_copy(
+            src_ref=outgo.at[spot],
+            dst_ref=duo.at[spot, slot],
+            send_sem=mate_send.at[spot],
+            recv_sem=mate_recv.at[spot],
+            device_id=(grp, mate),
+            device_id_type=MESH,
+        )
+
+    def up_copy(spot, shard, host):
+        return pltpu.make_async_remote_copy(
+            src_ref=comp.at[spot],
+            dst_ref=arrived.at[shard, lax.rem(spot, per)],
+            send_sem=up_send.at[spot],
+            recv_sem=up_recv.at[shard, lax.rem(spot, per)],
+            device_id=(grp, 2 * host + side),
+            device_id_type=MESH,
+        )
+
+    def for_mate(turn, _):
+        spots, steps = compute(turn, 1 - side)
+        for spot, step in zip(spots, steps):
+            outgo[spot] = step
+            mate_copy(spot, side).start()
+        return 0
+
+    lax.fori_loop(0, turns, for_mate, 0)
+
+    def for_pair(turn, _):
+        spots, steps = compute(turn, side)
+        for spot, step in zip(spots, steps):
+            duo[spot, side] = step
+        for spot in spots:
+            mate_copy(spot, 1 - side).wait_recv()
+        joined = [join(duo[spot, 1], duo[spot, 0]) for spot in spots]
+        for spot, (whole, added) in zip(spots, joined):
+            comp[spot, :, :size] = whole
+            comp[spot, :, size:] = added
+            host = lax.div(spot, per)
+
+            @pl.when(host != place)
+            def _():
+                up_copy(spot, place, host).start()
+
+            @pl.when(host == place)
+            def _():
+                arrived[place, lax.rem(spot, per)] = comp[spot]
+
+        return 0
+
+    lax.fori_loop(0, turns, for_pair, 0)
 
     rows = lax.broadcasted_iota(jnp.int32, (size, 2 * size), 0)
     cols = lax.broadcasted_iota(jnp.int32, (size, 2 * size), 1)
 
-    def join(late, early):
-        product = mul_wide(late[:, :size], early)
-        return product[:, :size], product[:, size:] + late[:, size:]
-
-    def apply(step, state):
-        return mul(step[:, :size], state) + step[:, size:]
-
     def total_copy(target):
         return pltpu.make_async_remote_copy(
-            src_ref=prior.at[count],
+            src_ref=prior.at[places],
             dst_ref=total_in,
             send_sem=total_send,
             recv_sem=total_recv,
@@ -262,13 +304,23 @@
             device_id_type=MESH,
         )
 
-    def down_copy(shard, owner):
+    def down_copy(shard, host):
         return pltpu.make_async_remote_copy(
             src_ref=starts.at[shard],
-            dst_ref=begin.at[pl.ds(owner * per, per)],
+            dst_ref=slots.at[0, pl.ds(host * per, per)],
             send_sem=down_send.at[shard],
-            recv_sem=down_recv.at[owner],
-            device_id=(grp, shard),
+            recv_sem=down_recv.at[host],
+            device_id=(grp, 2 * shard + side),
+            device_id_type=MESH,
+        )
+
+    def relay_copy(host):
+        return pltpu.make_async_remote_copy(
+            src_ref=slots.at[1 - side, pl.ds(host * per, per)],
+            dst_ref=begin.at[pl.ds(host * per, per)],
+            send_sem=relay_send.at[host],
+            recv_sem=relay_recv.at[host],
+            device_id=(grp, mate),
             device_id_type=MESH,
         )
 
@@ -277,10 +329,10 @@
             prior[0, index] = jnp.where(rows == cols, 1.0, 0.0).astype(F32)
 
         def advance(shard, _):
-            @pl.when(shard != me)
+            @pl.when(shard != place)
             def _():
                 for index in range(per):
-                    up_copy(me * per + index, shard, me).wait_recv()
+                    up_copy(place * per + index, shard, place).wait_recv()
 
             for index in range(per):
                 whole, added = join(arrived[shard, index], prior[shard, index])
@@ -288,7 +340,7 @@
                 prior[shard + 1, index, :, size:] = added
             return 0
 
-        lax.fori_loop(0, count, advance, 0)
+        lax.fori_loop(0, places, advance, 0)
 
         @pl.when(odd == 0)
         def _():
@@ -301,7 +353,7 @@
         @pl.when(odd == 1)
         def _():
             total_copy(grp).wait_recv()
-            both = [join(prior[count, index], total_in[index]) for index in range(per)]
+            both = [join(prior[places, index], total_in[index]) for index in range(per)]
 
             @pl.when(pair > 0)
             def _():
@@ -327,57 +379,76 @@
             entry[...] = pair_in[...]
 
         def give(step, _):
-            shard = lax.rem(me + 1 + step, count)
+            shard = lax.rem(place + 1 + step, places)
             for index in range(per):
                 starts[shard, index] = apply(prior[shard, index], entry[index])
 
-            @pl.when(shard != me)
-            def _():
-                down_copy(shard, me).start()
-
-            @pl.when(shard == me)
-            def _():
-                begin[pl.ds(me * per, per)] = starts[shard]
+            @pl.when(shard != place)
+            def _():
+                down_copy(shard, place).start()
+
+            @pl.when(shard == place)
+            def _():
+                slots[0, pl.ds(place * per, per)] = starts[shard]
 
             return 0
 
-        lax.fori_loop(0, count, give, 0)
+        lax.fori_loop(0, places, give, 0)
 
     when_owner(compose)
     gate_copy.wait()
 
     def store(owner):
-        span = pl.ds(pl.multiple_of(owner * (per * size), per * size), per * size)
+        span = owner_columns(owner)
         return pltpu.make_async_copy(o_ref.at[:, span], o_hbm.at[:, span], store_sem.at[owner])
 
-    def finish(step, _):
-        owner = lax.rem(me + owners - step, owners) if everyone else step
-
-        @pl.when(owner != me)
-        def _():
-            down_copy(me, owner).wait_recv()
-
+    def finish(owner, states):
         for index in range(per):
             head = owner * per + index
-            raw = mul(reach[head], begin[head]) + local[head]
+            raw = mul(reach[head], states[index]) + local[head]
             scaled = raw * lax.rsqrt(jnp.mean(raw * raw, axis=-1, keepdims=True) + 1e-05)
             gate = g_ref[:, columns(head)].astype(F32)
             o_ref[:, columns(head)] = (scaled / (1.0 + jnp.exp(-gate))).astype(BF16)
         store(owner).start()
-        return 0
-
-    lax.fori_loop(0, owners, finish, 0)
-
-    def drain_up(head, _):
-        owner = lax.div(head, per)
-
-        @pl.when(owner != me)
-        def _():
-            up_copy(head, me, owner).wait_send()
-
-        return 0
-
-    lax.fori_loop(0, heads, drain_up, 0)
+
+    def nearest(step):
+        return lax.rem(place + hosts - step, hosts) if everyone else step
+
+    def relay(step, _):
+        host = nearest(step)
+
+        @pl.when(host != place)
+        def _():
+            down_copy(place, host).wait_recv()
+
+        for index in range(per):
+            spot = host * per + index
+            slots[1, spot] = apply(duo[spot, 0], slots[0, spot])
+        relay_copy(host).start()
+        finish(2 * host + side, [slots[side, host * per + index] for index in range(per)])
+        return 0
+
+    lax.fori_loop(0, hosts, relay, 0)
+
+    def last(step, _):
+        host = nearest(step)
+        relay_copy(host).wait_recv()
+        finish(2 * host + 1 - side, [begin[host * per + index] for index in range(per)])
+        return 0
+
+    lax.fori_loop(0, hosts, last, 0)
+
+    def drain(spot, _):
+        mate_copy(spot, side).wait_send()
+        host = lax.div(spot, per)
+
+        @pl.when(host != place)
+        def _():
+            up_copy(spot, place, host).wait_send()
+
+        return 0
+
+    lax.fori_loop(0, heads // 2, drain, 0)
 
     def drain_down():
         @pl.when(odd == 0)
@@ -390,15 +461,21 @@
             pair_copy(1).wait_send()
 
         def one(shard, _):
-            @pl.when(shard != me)
-            def _():
-                down_copy(shard, me).wait_send()
+            @pl.when(shard != place)
+            def _():
+                down_copy(shard, place).wait_send()
 
             return 0
 
-        lax.fori_loop(0, count, one, 0)
+        lax.fori_loop(0, places, one, 0)
 
     when_owner(drain_down)
+
+    def drain_relay(host, _):
+        relay_copy(host).wait_send()
+        return 0
+
+    lax.fori_loop(0, hosts, drain_relay, 0)
 
     def drain_store(owner, _):
         store(owner).wait()
@@ -412,6 +489,8 @@
     heads = write_rate.shape[1]
     size = features // heads
     per = max(heads // count, 1)
+    owners = heads // per
+    half, places, hosts = heads // 2, count // 2, owners // 2
     dma = pltpu.SemaphoreType.DMA
     square = (size, size)
     wide = (size, 2 * size)
@@ -423,31 +502,38 @@
         out_specs=pl.BlockSpec(memory_space=pltpu.HBM),
         scratch_shapes=[pltpu.VMEM((local_len, features), BF16)] * 6
         + [
-            pltpu.VMEM((heads, *wide), F32),
-            pltpu.VMEM((count, per, *wide), F32),
-            pltpu.VMEM((count + 1, per, *wide), F32),
+            pltpu.VMEM((half, *wide), F32),
+            pltpu.VMEM((half, 2, *wide), F32),
+            pltpu.VMEM((half, *wide), F32),
+            pltpu.VMEM((places, per, *wide), F32),
+            pltpu.VMEM((places + 1, per, *wide), F32),
             pltpu.VMEM((per, *wide), F32),
             pltpu.VMEM((per, *square), F32),
             pltpu.VMEM((per, *square), F32),
             pltpu.VMEM((per, *square), F32),
-            pltpu.VMEM((count, per, *square), F32),
-            pltpu.VMEM((heads, *square), F32),
+            pltpu.VMEM((places, per, *square), F32),
+            pltpu.VMEM((2, half, *square), F32),
+            pltpu.VMEM((half, *square), F32),
             pltpu.VMEM((heads, local_len, size), F32),
             pltpu.VMEM((heads, local_len, size), F32),
-            dma((4, heads // BATCH)),
+            dma((4, owners)),
             dma,
-            dma((heads // per,)),
-            dma((heads,)),
-            dma((count, per)),
+            dma((owners,)),
+            dma((half,)),
+            dma((half,)),
+            dma((half,)),
+            dma((places, per)),
             dma,
             dma,
             dma((2,)),
             dma,
-            dma((count,)),
-            dma((heads // per,)),
+            dma((places,)),
+            dma((hosts,)),
+            dma((hosts,)),
+            dma((hosts,)),
         ],
         compiler_params=pltpu.CompilerParams(
-            collective_id=0, has_side_effects=True, vmem_limit_bytes=48 * 1024 * 1024
+            collective_id=0, has_side_effects=True, vmem_limit_bytes=63 * 1024 * 1024
         ),
         name="delta_attention",
     )

time: 98.7 us -> 71.6 us (0.73)
  the two profiles are of different devices: /device:TPU:22 before, /device:TPU:18 now
where the time goes in v2:
time: 71.6 us; the launch traced here: 71.4 us
  Pallas kernels  69.5 us (97%)
  local copies, waits for them, and re-layouts  1.88 us (3%)
    pallas_call x1, Pallas kernels, shards(): call(queries[0], key_vectors[0], values[0], log_decay[0], out_gate[0], wr...  69.5 us
    unnamed x1, local copies, waits for them, and re-layouts  1.88 us

profile of v2, /device:TPU:18, one launch (start us, length us, event | category | flops | bytes accessed | tf_op | source)
XLA Modules:
  0.0 71.4 jit_solution(14633279872656818938)
XLA Ops:
  0.0 69.5 %delta_attention.1 = bf16[128,2048]{1,0:T(8,128)(2,1)} custom-call(bf16[128,2048]{1,0:T(8,128)(2,1)} %bitcast.8, bf16[128,2048]{1,0:T(8,128)(2,1)} %bitcast.9, bf16[128,2048]{1,0:T(8,128)(2,1)} %bitcast.10, bf16[128,2048]{1,0:T(8,128)(2,1)} %bitcast.11, bf16[128,2048]{1,0:T(8,128)(2,1)} %bitcast.12, f32[16,128]{1,0:T(8,128)} %bitcast.13), custom_call_target="tpu_custom_call" | custom-call | tf_op jit(solution)/shard_map/delta_attention/pallas_call | solution.py:540
  69.5 1.9 %copy.8 = bf16[1,128,2048]{2,1,0:T(8,128)(2,1)} copy(bf16[1,128,2048]{2,1,0:T(8,128)(2,1)} %bitcast.7) | data formatting | bytes 1048576

commit v3 on v2

--- a/solution.py
+++ b/solution.py
@@ -23,6 +23,17 @@
     lhs = jnp.concatenate(split(left), axis=1)
     parts = jnp.concatenate(split(right), axis=1)
     out = jnp.dot(lhs, jnp.concatenate([parts, parts], axis=0), preferred_element_type=F32)
+    return out[:, :width] + out[:, width:]
+
+
+def mul_split(left, right):
+    width = right[0].shape[1]
+    parts = jnp.concatenate(right, axis=1)
+    out = jnp.dot(
+        jnp.concatenate(left, axis=1),
+        jnp.concatenate([parts, parts], axis=0),
+        preferred_element_type=F32,
+    )
     return out[:, :width] + out[:, width:]
 
 
@@ -45,8 +56,18 @@
     )
 
 
-def local_terms(queries, keys, values, decays, rates):
-    extent, size = queries[0].shape
+def mul_both(upper, lower, right):
+    width = right[0].shape[1]
+    lhs = jnp.concatenate(
+        [jnp.concatenate([up, low], axis=0) for up, low in zip(upper, lower)], axis=1
+    )
+    parts = jnp.concatenate(right, axis=1)
+    out = jnp.dot(lhs, jnp.concatenate([parts, parts], axis=0), preferred_element_type=F32)
+    return out[:, :width] + out[:, width:]
+
+
+def state_terms(keys, values, decays, rates):
+    extent, size = keys[0].shape
     half = extent // 2
     rows = lax.broadcasted_iota(jnp.int32, (extent, extent), 0)
     cols = lax.broadcasted_iota(jnp.int32, (extent, extent), 1)
@@ -54,68 +75,69 @@
     eye = jnp.where(rows == cols, 1.0, 0.0).astype(F32)
     ones = jnp.where(rows >= cols, 1.0, 0.0).astype(BF16)
     cums = [jnp.dot(ones, decay, preferred_element_type=F32) for decay in decays]
-    q_f = [query.astype(F32) for query in queries]
     units = []
     for key in keys:
         key_f = key.astype(F32)
         units.append(key_f * lax.rsqrt(jnp.sum(key_f * key_f, axis=-1, keepdims=True) + 1e-06))
-    pairs = []
-    for query, unit, cum in zip(q_f, units, cums):
-        middle = cum[half - 1 : half]
-        grow = jnp.exp(cum - middle)
-        pairs.append(
-            mul_rows(
-                jnp.concatenate([unit * grow, query * grow], axis=0), unit * jnp.exp(middle - cum)
-            )
-        )
-    lowers, attends = [], []
-    for pair, rate in zip(pairs, rates):
-        lowers.append(jnp.where(rows > cols, pair[:extent] * rate, 0.0))
-        attends.append(jnp.where(rows >= cols, pair[extent:] * rate, 0.0))
+    shrunk = [unit * jnp.exp(cum[half - 1 : half] - cum) for unit, cum in zip(units, cums)]
+    pairs = [
+        mul_rows(unit * jnp.exp(cum - cum[half - 1 : half]), shrink)
+        for unit, cum, shrink in zip(units, cums, shrunk)
+    ]
+    lowers = [jnp.where(rows > cols, product * rate, 0.0) for product, rate in zip(pairs, rates)]
     diag = [jnp.where(same, lower, 0.0) for lower in lowers]
     below = [jnp.where(same, 0.0, lower) for lower in lowers]
     inverse = [eye - part for part in diag]
-    power = [mul(part, part) for part in diag]
+    power = [split(mul(part, part)) for part in diag]
     for _ in range(half.bit_length() - 3):
-        both = [mul(jnp.concatenate([x, p], axis=0), p) for x, p in zip(inverse, power)]
+        both = [mul_both(split(x), p, p) for x, p in zip(inverse, power)]
         inverse = [x + b[:extent] for x, b in zip(inverse, both)]
-        power = [b[extent:] for b in both]
-    inverse = [x + mul(x, p) for x, p in zip(inverse, power)]
+        power = [split(b[extent:]) for b in both]
+    inverse = [x + mul_split(split(x), p) for x, p in zip(inverse, power)]
     corner = [mul(x[half:], c) for x, c in zip(inverse, below)]
     corner = [mul(c, x) for c, x in zip(corner, inverse)]
     inverse = [
         jnp.concatenate([x[:half], x[half:] - c], axis=0) for x, c in zip(inverse, corner)
     ]
-    from_start = [jnp.exp(cum) for cum in cums]
     carry = [
-        mul_wide(x, jnp.concatenate([unit * grow, value.astype(F32)], axis=1))
-        for x, unit, grow, value in zip(inverse, units, from_start, values)
+        mul_wide(x, jnp.concatenate([unit * jnp.exp(cum), value.astype(F32)], axis=1))
+        for x, unit, cum, value in zip(inverse, units, cums, values)
     ]
-    results = []
-    for query, unit, cum, grow, attend, rate, carried in zip(
-        q_f, units, cums, from_start, attends, rates, carry
-    ):
+    steps = []
+    for unit, cum, rate, carried in zip(units, cums, rates, carry):
         last = cum[extent - 1 : extent]
         key_end = jnp.transpose(unit * jnp.exp(last - cum)) * rate
-        out = mul_wide(jnp.concatenate([attend, key_end], axis=0), carried)
-        step_map = jnp.where(rows == cols, jnp.exp(last), 0.0) - out[extent:, :size]
-        results.append(
-            (
-                query * grow - out[:extent, :size],
-                out[:extent, size:],
-                jnp.concatenate([step_map, out[extent:, size:]], axis=1),
-            )
-        )
-    return results
+        out = mul_wide(key_end, carried)
+        step_map = jnp.where(rows == cols, jnp.exp(last), 0.0) - out[:, :size]
+        steps.append(jnp.concatenate([step_map, out[:, size:]], axis=1))
+    return cums, shrunk, carry, steps
+
+
+def output_terms(queries, cums, shrunk, carry, rates):
+    extent, size = queries[0].shape
+    half = extent // 2
+    rows = lax.broadcasted_iota(jnp.int32, (extent, extent), 0)
+    cols = lax.broadcasted_iota(jnp.int32, (extent, extent), 1)
+    q_f = [query.astype(F32) for query in queries]
+    pairs = [
+        mul_rows(query * jnp.exp(cum - cum[half - 1 : half]), shrink)
+        for query, cum, shrink in zip(q_f, cums, shrunk)
+    ]
+    attends = [jnp.where(rows >= cols, product * rate, 0.0) for product, rate in zip(pairs, rates)]
+    outs = [mul_wide(attend, carried) for attend, carried in zip(attends, carry)]
+    return [
+        (query * jnp.exp(cum) - out[:, :size], out[:, size:])
+        for query, cum, out in zip(q_f, cums, outs)
+    ]
 
 
 def kernel(
     groups, count, heads,
-    q_hbm, k_hbm, v_hbm, d_hbm, g_hbm, r_ref, o_hbm,
-    q_ref, k_ref, v_ref, d_ref, g_ref, o_ref,
+    q_hbm, k_hbm, v_hbm, d_hbm, g_hbm, r_ref, o_ref,
+    q_ref, k_ref, v_ref, d_ref, g_ref,
     outgo, duo, comp, arrived, prior, total_in, pair_in, entry, onward, starts, slots, begin,
-    reach, local,
-    load_sem, gate_sem, store_sem, mate_send, mate_recv, up_send, up_recv,
+    reach, local, kept_cum, kept_key, kept_carry,
+    load_sem, query_sem, gate_sem, mate_send, mate_recv, up_send, up_recv,
     total_send, total_recv, pair_send, pair_recv, down_send, down_recv, relay_send, relay_recv,
 ):
     grp, me = lax.axis_index("grp"), lax.axis_index("seq")
@@ -183,7 +205,7 @@
         return [
             pltpu.make_async_copy(far.at[:, span], near.at[:, span], load_sem.at[index, owner])
             for index, (far, near) in enumerate(
-                [(d_hbm, d_ref), (k_hbm, k_ref), (q_hbm, q_ref), (v_hbm, v_ref)]
+                [(d_hbm, d_ref), (k_hbm, k_ref), (v_hbm, v_ref)]
             )
         ]
 
@@ -192,6 +214,8 @@
             for owner in turn_owners(turn, whose):
                 for copy in load(owner):
                     copy.start()
+    query_copy = pltpu.make_async_copy(q_hbm, q_ref, query_sem)
+    query_copy.start()
     gate_copy = pltpu.make_async_copy(g_hbm, g_ref, gate_sem)
     gate_copy.start()
 
@@ -216,17 +240,31 @@
         picked = [owner * per + index for owner in turn_of for index in range(per)]
         places_in = [lax.div(owner, 2) * per + index for owner in turn_of for index in range(per)]
         spans = [columns(head) for head in picked]
-        results = local_terms(
-            [q_ref[:, span] for span in spans],
+        cums, shrunk, carry, steps = state_terms(
             [k_ref[:, span] for span in spans],
             [v_ref[:, span] for span in spans],
             [d_ref[:, span] for span in spans],
             [r_ref[pl.ds(head, 1), :] for head in picked],
         )
-        for head, (head_reach, head_local, _step) in zip(picked, results):
+        for head, cum, shrink, carried in zip(picked, cums, shrunk, carry):
+            kept_cum[head] = cum
+            kept_key[head] = shrink
+            kept_carry[head] = carried
+        return places_in, steps
+
+    def outputs(batch, _):
+        picked = [batch * BATCH + index for index in range(BATCH)]
+        results = output_terms(
+            [q_ref[:, columns(head)] for head in picked],
+            [kept_cum[head] for head in picked],
+            [kept_key[head] for head in picked],
+            [kept_carry[head] for head in picked],
+            [r_ref[pl.ds(head, 1), :] for head in picked],
+        )
+        for head, (head_reach, head_local) in zip(picked, results):
             reach[head] = head_reach
             local[head] = head_local
-        return places_in, [result[2] for result in results]
+        return 0
 
     def mate_copy(spot, slot):
         return pltpu.make_async_remote_copy(
@@ -395,12 +433,12 @@
 
         lax.fori_loop(0, places, give, 0)
 
+    batches = heads // BATCH
+    query_copy.wait()
+    lax.fori_loop(0, batches // 2, outputs, 0)
     when_owner(compose)
+    lax.fori_loop(batches // 2, batches, outputs, 0)
     gate_copy.wait()
-
-    def store(owner):
-        span = owner_columns(owner)
-        return pltpu.make_async_copy(o_ref.at[:, span], o_hbm.at[:, span], store_sem.at[owner])
 
     def finish(owner, states):
         for index in range(per):
@@ -409,7 +447,6 @@
             scaled = raw * lax.rsqrt(jnp.mean(raw * raw, axis=-1, keepdims=True) + 1e-05)
             gate = g_ref[:, columns(head)].astype(F32)
             o_ref[:, columns(head)] = (scaled / (1.0 + jnp.exp(-gate))).astype(BF16)
-        store(owner).start()
 
     def nearest(step):
         return lax.rem(place + hosts - step, hosts) if everyone else step
@@ -476,12 +513,6 @@
         return 0
 
     lax.fori_loop(0, hosts, drain_relay, 0)
-
-    def drain_store(owner, _):
-        store(owner).wait()
-        return 0
-
-    lax.fori_loop(0, owners, drain_store, 0)
 
 
 def shards(groups, count, queries, key_vectors, values, log_decay, write_rate, out_gate):
@@ -499,8 +530,8 @@
         out_shape=jax.ShapeDtypeStruct((local_len, features), BF16),
         in_specs=[pl.BlockSpec(memory_space=pltpu.HBM)] * 5
         + [pl.BlockSpec(memory_space=pltpu.VMEM)],
-        out_specs=pl.BlockSpec(memory_space=pltpu.HBM),
-        scratch_shapes=[pltpu.VMEM((local_len, features), BF16)] * 6
+        out_specs=pl.BlockSpec(memory_space=pltpu.VMEM),
+        scratch_shapes=[pltpu.VMEM((local_len, features), BF16)] * 5
         + [
             pltpu.VMEM((half, *wide), F32),
             pltpu.VMEM((half, 2, *wide), F32),
@@ -516,9 +547,12 @@
             pltpu.VMEM((half, *square), F32),
             pltpu.VMEM((heads, local_len, size), F32),
             pltpu.VMEM((heads, local_len, size), F32),
-            dma((4, owners)),
+            pltpu.VMEM((heads, local_len, size), F32),
+            pltpu.VMEM((heads, local_len, size), F32),
+            pltpu.VMEM((heads, local_len, 2 * size), F32),
+            dma((3, owners)),
             dma,
-            dma((owners,)),
+            dma,
             dma((half,)),
             dma((half,)),
             dma((half,)),

time: 71.6 us -> 71.6 us (level)
  no operation moved by 1% of the time
where the time goes in v3:
time: 71.6 us; the launch traced here: 71.4 us
  Pallas kernels  69.5 us (97%)
  local copies, waits for them, and re-layouts  1.88 us (3%)
    pallas_call x1, Pallas kernels, shards(): call(queries[0], key_vectors[0], values[0], log_decay[0], out_gate[0], wr...  69.5 us
    unnamed x1, local copies, waits for them, and re-layouts  1.88 us

profile of v3, /device:TPU:18, one launch (start us, length us, event | category | flops | bytes accessed | tf_op | source)
XLA Modules:
  0.0 71.4 jit_solution(3806642828533193955)
XLA Ops:
  0.0 69.5 %delta_attention.1 = bf16[128,2048]{1,0:T(8,128)(2,1)} custom-call(bf16[128,2048]{1,0:T(8,128)(2,1)} %bitcast.8, bf16[128,2048]{1,0:T(8,128)(2,1)} %bitcast.9, bf16[128,2048]{1,0:T(8,128)(2,1)} %bitcast.10, bf16[128,2048]{1,0:T(8,128)(2,1)} %bitcast.11, bf16[128,2048]{1,0:T(8,128)(2,1)} %bitcast.12, f32[16,128]{1,0:T(8,128)} %bitcast.13), custom_call_target="tpu_custom_call" | custom-call | tf_op jit(solution)/shard_map/delta_attention/pallas_call | solution.py:574
  69.5 1.9 %copy.8 = bf16[1,128,2048]{2,1,0:T(8,128)(2,1)} copy(bf16[1,128,2048]{2,1,0:T(8,128)(2,1)} %bitcast.7) | data formatting | bytes 1048576

commit v4 on v3

--- a/solution.py
+++ b/solution.py
@@ -7,7 +7,7 @@
 from jax.sharding import PartitionSpec as P
 
 BLOCK = 64
-BATCH = 4
+BATCH = 2
 MESH = pl.DeviceIdType.MESH
 F32 = jnp.float32
 BF16 = jnp.bfloat16
@@ -131,6 +131,23 @@
     ]
 
 
+def flip(own, high, low):
+    return 2 * lax.rem(lax.div(own, 2) + high, 2) + lax.rem(lax.rem(own, 2) + low, 2)
+
+
+def far_first(step, own, extent):
+    if extent != 4:
+        return lax.rem(own + 1 + step, extent)
+    late = lax.div(step, 2)
+    return flip(own, 1 - late, lax.rem(step + late, 2))
+
+
+def near_first(step, own, extent):
+    if extent != 4:
+        return lax.rem(own + extent - step, extent)
+    return flip(own, lax.div(step, 2), lax.rem(step, 2))
+
+
 def kernel(
     groups, count, heads,
     q_hbm, k_hbm, v_hbm, d_hbm, g_hbm, r_ref, o_ref,
@@ -150,7 +167,7 @@
     mate = me + 1 - 2 * side
     turns = heads // 2 // BATCH
     runs = BATCH // per
-    first_turn = lax.div(per * place, BATCH) + 1
+    own_turn = lax.rem(lax.div(per * place, BATCH), turns)
     pair, odd = lax.div(grp, 2), lax.rem(grp, 2)
     last_pair = groups // 2 - 1
 
@@ -194,7 +211,7 @@
         greet_at(grp + 2, me)
 
     def turn_owners(turn, whose):
-        start = lax.rem(turn + first_turn, turns) * runs
+        start = far_first(jnp.int32(turn), own_turn, turns) * runs
         return [2 * (start + run) + whose for run in range(runs)]
 
     def owner_columns(owner):
@@ -252,8 +269,10 @@
             kept_carry[head] = carried
         return places_in, steps
 
-    def outputs(batch, _):
-        picked = [batch * BATCH + index for index in range(BATCH)]
+    def outputs(turn, whose):
+        picked = [
+            owner * per + index for owner in turn_owners(turn, whose) for index in range(per)
+        ]
         results = output_terms(
             [q_ref[:, columns(head)] for head in picked],
             [kept_cum[head] for head in picked],
@@ -264,7 +283,6 @@
         for head, (head_reach, head_local) in zip(picked, results):
             reach[head] = head_reach
             local[head] = head_local
-        return 0
 
     def mate_copy(spot, slot):
         return pltpu.make_async_remote_copy(
@@ -315,8 +333,10 @@
             def _():
                 arrived[place, lax.rem(spot, per)] = comp[spot]
 
-        return 0
-
+        outputs(turn, 1 - side)
+        return 0
+
+    query_copy.wait()
     lax.fori_loop(0, turns, for_pair, 0)
 
     rows = lax.broadcasted_iota(jnp.int32, (size, 2 * size), 0)
@@ -417,7 +437,7 @@
             entry[...] = pair_in[...]
 
         def give(step, _):
-            shard = lax.rem(place + 1 + step, places)
+            shard = far_first(step, place, places)
             for index in range(per):
                 starts[shard, index] = apply(prior[shard, index], entry[index])
 
@@ -433,11 +453,13 @@
 
         lax.fori_loop(0, places, give, 0)
 
-    batches = heads // BATCH
-    query_copy.wait()
-    lax.fori_loop(0, batches // 2, outputs, 0)
     when_owner(compose)
-    lax.fori_loop(batches // 2, batches, outputs, 0)
+
+    def own_outputs(turn, _):
+        outputs(turn, side)
+        return 0
+
+    lax.fori_loop(0, turns, own_outputs, 0)
     gate_copy.wait()
 
     def finish(owner, states):
@@ -449,7 +471,7 @@
             o_ref[:, columns(head)] = (scaled / (1.0 + jnp.exp(-gate))).astype(BF16)
 
     def nearest(step):
-        return lax.rem(place + hosts - step, hosts) if everyone else step
+        return near_first(step, place, hosts) if everyone else step
 
     def relay(step, _):
         host = nearest(step)

time: 71.6 us -> 68.5 us (0.957)
  the two profiles are of different devices: /device:TPU:18 before, /device:TPU:14 now
where the time goes in v4:
time: 68.5 us; the launch traced here: 67.3 us
  Pallas kernels  65.4 us (95%)
  local copies, waits for them, and re-layouts  1.88 us (3%)
    pallas_call x1, Pallas kernels, shards(): call(queries[0], key_vectors[0], values[0], log_decay[0], out_gate[0], wr...  65.4 us
    unnamed x1, local copies, waits for them, and re-layouts  1.88 us

profile of v4, /device:TPU:14, one launch (start us, length us, event | category | flops | bytes accessed | tf_op | source)
XLA Modules:
  0.0 67.3 jit_solution(9167862544369630475)
XLA Ops:
  0.0 65.4 %delta_attention.1 = bf16[128,2048]{1,0:T(8,128)(2,1)} custom-call(bf16[128,2048]{1,0:T(8,128)(2,1)} %bitcast.8, bf16[128,2048]{1,0:T(8,128)(2,1)} %bitcast.9, bf16[128,2048]{1,0:T(8,128)(2,1)} %bitcast.10, bf16[128,2048]{1,0:T(8,128)(2,1)} %bitcast.11, bf16[128,2048]{1,0:T(8,128)(2,1)} %bitcast.12, f32[16,128]{1,0:T(8,128)} %bitcast.13), custom_call_target="tpu_custom_call" | custom-call | tf_op jit(solution)/shard_map/delta_attention/pallas_call | solution.py:596
  65.4 1.9 %copy.8 = bf16[1,128,2048]{2,1,0:T(8,128)(2,1)} copy(bf16[1,128,2048]{2,1,0:T(8,128)(2,1)} %bitcast.7) | data formatting | bytes 1048576

commit v5 on v4

--- a/solution.py
+++ b/solution.py
@@ -226,8 +226,8 @@
             )
         ]
 
-    for whose in (1 - side, side):
-        for turn in range(turns):
+    for turn in range(turns):
+        for whose in (1 - side, side):
             for owner in turn_owners(turn, whose):
                 for copy in load(owner):
                     copy.start()
@@ -249,13 +249,19 @@
     def apply(step, state):
         return mul(step[:, :size], state) + step[:, size:]
 
-    def compute(turn, whose):
-        turn_of = turn_owners(turn, whose)
+    def turn_spots(turn):
+        return [
+            lax.div(owner, 2) * per + index
+            for owner in turn_owners(turn, side)
+            for index in range(per)
+        ]
+
+    def compute(turn):
+        turn_of = turn_owners(turn, 1 - side) + turn_owners(turn, side)
         for owner in turn_of:
             for copy in load(owner):
                 copy.wait()
         picked = [owner * per + index for owner in turn_of for index in range(per)]
-        places_in = [lax.div(owner, 2) * per + index for owner in turn_of for index in range(per)]
         spans = [columns(head) for head in picked]
         cums, shrunk, carry, steps = state_terms(
             [k_ref[:, span] for span in spans],
@@ -267,7 +273,7 @@
             kept_cum[head] = cum
             kept_key[head] = shrink
             kept_carry[head] = carried
-        return places_in, steps
+        return steps
 
     def outputs(turn, whose):
         picked = [
@@ -304,19 +310,8 @@
             device_id_type=MESH,
         )
 
-    def for_mate(turn, _):
-        spots, steps = compute(turn, 1 - side)
-        for spot, step in zip(spots, steps):
-            outgo[spot] = step
-            mate_copy(spot, side).start()
-        return 0
-
-    lax.fori_loop(0, turns, for_mate, 0)
-
-    def for_pair(turn, _):
-        spots, steps = compute(turn, side)
-        for spot, step in zip(spots, steps):
-            duo[spot, side] = step
+    def pair_up(turn):
+        spots = turn_spots(turn)
         for spot in spots:
             mate_copy(spot, 1 - side).wait_recv()
         joined = [join(duo[spot, 1], duo[spot, 0]) for spot in spots]
@@ -333,11 +328,24 @@
             def _():
                 arrived[place, lax.rem(spot, per)] = comp[spot]
 
-        outputs(turn, 1 - side)
+    def first_phase(turn, _):
+        spots = turn_spots(turn)
+        steps = compute(turn)
+        for spot, step in zip(spots, steps[:BATCH]):
+            outgo[spot] = step
+            mate_copy(spot, side).start()
+        for spot, step in zip(spots, steps[BATCH:]):
+            duo[spot, side] = step
+
+        @pl.when(turn > 0)
+        def _():
+            pair_up(turn - 1)
+
         return 0
 
+    lax.fori_loop(0, turns, first_phase, 0)
+    pair_up(turns - 1)
     query_copy.wait()
-    lax.fori_loop(0, turns, for_pair, 0)
 
     rows = lax.broadcasted_iota(jnp.int32, (size, 2 * size), 0)
     cols = lax.broadcasted_iota(jnp.int32, (size, 2 * size), 1)
@@ -475,6 +483,10 @@
 
     def relay(step, _):
         host = nearest(step)
+
+        @pl.when(step < turns)
+        def _():
+            outputs(step, 1 - side)
 
         @pl.when(host != place)
         def _():

time: 68.5 us -> 65.9 us (0.962); the launches traced: 67.3 us -> 65.8 us
  Pallas kernels: 65.4 us -> 63.9 us
    pallas_call x1, Pallas kernels: 65.4 us -> 63.9 us  [shards(): call(queries[0], key_vectors[0], values[0], log_decay[0], out_gate[0], wr...]
where the time goes in v5:
time: 65.9 us; the launch traced here: 65.8 us
  Pallas kernels  63.9 us (97%)
  local copies, waits for them, and re-layouts  1.88 us (3%)
    pallas_call x1, Pallas kernels, shards(): call(queries[0], key_vectors[0], values[0], log_decay[0], out_gate[0], wr...  63.9 us
    unnamed x1, local copies, waits for them, and re-layouts  1.88 us

profile of v5, /device:TPU:14, one launch (start us, length us, event | category | flops | bytes accessed | tf_op | source)
XLA Modules:
  0.0 65.8 jit_solution(10496878141868246306)
XLA Ops:
  0.0 63.9 %delta_attention.1 = bf16[128,2048]{1,0:T(8,128)(2,1)} custom-call(bf16[128,2048]{1,0:T(8,128)(2,1)} %bitcast.8, bf16[128,2048]{1,0:T(8,128)(2,1)} %bitcast.9, bf16[128,2048]{1,0:T(8,128)(2,1)} %bitcast.10, bf16[128,2048]{1,0:T(8,128)(2,1)} %bitcast.11, bf16[128,2048]{1,0:T(8,128)(2,1)} %bitcast.12, f32[16,128]{1,0:T(8,128)} %bitcast.13), custom_call_target="tpu_custom_call" | custom-call | tf_op jit(solution)/shard_map/delta_attention/pallas_call | solution.py:608
  63.9 1.9 %copy.8 = bf16[1,128,2048]{2,1,0:T(8,128)(2,1)} copy(bf16[1,128,2048]{2,1,0:T(8,128)(2,1)} %bitcast.7) | data formatting | bytes 1048576

commit v6 on v5

--- a/solution.py
+++ b/solution.py
@@ -347,6 +347,12 @@
     pair_up(turns - 1)
     query_copy.wait()
 
+    def mate_outputs(turn, _):
+        outputs(turn, 1 - side)
+        return 0
+
+    lax.fori_loop(0, turns, mate_outputs, 0)
+
     rows = lax.broadcasted_iota(jnp.int32, (size, 2 * size), 0)
     cols = lax.broadcasted_iota(jnp.int32, (size, 2 * size), 1)
 
@@ -483,10 +489,6 @@
 
     def relay(step, _):
         host = nearest(step)
-
-        @pl.when(step < turns)
-        def _():
-            outputs(step, 1 - side)
 
         @pl.when(host != place)
         def _():

time: 65.9 us -> 65.9 us (level)
  no operation moved by 1% of the time
where the time goes in v6:
time: 65.9 us; the launch traced here: 65.8 us
  Pallas kernels  63.9 us (97%)
  local copies, waits for them, and re-layouts  1.88 us (3%)
    pallas_call x1, Pallas kernels, shards(): call(queries[0], key_vectors[0], values[0], log_decay[0], out_gate[0], wr...  63.9 us
    unnamed x1, local copies, waits for them, and re-layouts  1.88 us

profile of v6, /device:TPU:14, one launch (start us, length us, event | category | flops | bytes accessed | tf_op | source)
XLA Modules:
  0.0 65.8 jit_solution(5056215341082343424)
XLA Ops:
  0.0 63.9 %delta_attention.1 = bf16[128,2048]{1,0:T(8,128)(2,1)} custom-call(bf16[128,2048]{1,0:T(8,128)(2,1)} %bitcast.8, bf16[128,2048]{1,0:T(8,128)(2,1)} %bitcast.9, bf16[128,2048]{1,0:T(8,128)(2,1)} %bitcast.10, bf16[128,2048]{1,0:T(8,128)(2,1)} %bitcast.11, bf16[128,2048]{1,0:T(8,128)(2,1)} %bitcast.12, f32[16,128]{1,0:T(8,128)} %bitcast.13), custom_call_target="tpu_custom_call" | custom-call | tf_op jit(solution)/shard_map/delta_attention/pallas_call | solution.py:610
  63.9 1.9 %copy.8 = bf16[1,128,2048]{2,1,0:T(8,128)(2,1)} copy(bf16[1,128,2048]{2,1,0:T(8,128)(2,1)} %bitcast.7) | data formatting | bytes 1048576

commit v7 on v5

--- a/solution.py
+++ b/solution.py
@@ -461,13 +461,13 @@
 
         lax.fori_loop(0, places, give, 0)
 
-    when_owner(compose)
-
     def own_outputs(turn, _):
         outputs(turn, side)
         return 0
 
     lax.fori_loop(0, turns, own_outputs, 0)
+    when_owner(compose)
+
     gate_copy.wait()
 
     def finish(owner, states):

time: 65.9 us -> 66 us (level)
  no operation moved by 1% of the time
where the time goes in v7:
time: 66 us; the launch traced here: 65.8 us
  Pallas kernels  63.9 us (97%)
  local copies, waits for them, and re-layouts  1.88 us (3%)
    pallas_call x1, Pallas kernels, shards(): call(queries[0], key_vectors[0], values[0], log_decay[0], out_gate[0], wr...  63.9 us
    unnamed x1, local copies, waits for them, and re-layouts  1.88 us

profile of v7, /device:TPU:14, one launch (start us, length us, event | category | flops | bytes accessed | tf_op | source)
XLA Modules:
  0.0 65.8 jit_solution(9610362754225024159)
XLA Ops:
  0.0 63.9 %delta_attention.1 = bf16[128,2048]{1,0:T(8,128)(2,1)} custom-call(bf16[128,2048]{1,0:T(8,128)(2,1)} %bitcast.8, bf16[128,2048]{1,0:T(8,128)(2,1)} %bitcast.9, bf16[128,2048]{1,0:T(8,128)(2,1)} %bitcast.10, bf16[128,2048]{1,0:T(8,128)(2,1)} %bitcast.11, bf16[128,2048]{1,0:T(8,128)(2,1)} %bitcast.12, f32[16,128]{1,0:T(8,128)} %bitcast.13), custom_call_target="tpu_custom_call" | custom-call | tf_op jit(solution)/shard_map/delta_attention/pallas_call | solution.py:608
  63.9 1.9 %copy.8 = bf16[1,128,2048]{2,1,0:T(8,128)(2,1)} copy(bf16[1,128,2048]{2,1,0:T(8,128)(2,1)} %bitcast.7) | data formatting | bytes 1048576
